TPU v7x, 32 devices: a whole 2x2x4 slice. The times are simulated.
32 devices in a mesh: blk: 16 (over z, x, core), group: 2 (over y).
Axes of the slice: x: 2, y: 2, z: 4, core: 2. Of those that a mesh axis runs over, the one named last changes fastest.
Arguments:
- audio_features: bfloat16 [4096, 768], P(('blk', 'group')), may hold values from -6 to 6
- audio_weight: bfloat16 [768, 512], replicated, may hold values from -0.21875 to 0.21875
- text_features: bfloat16 [4096, 768], P(('blk', 'group')), may hold values from -6 to 6
- text_weight: bfloat16 [768, 512], replicated, may hold values from -0.21875 to 0.21875
- logit_scale: float32 [1], replicated, may hold values from 10 to 30
- logit_bias: float32 [1], replicated, may hold values from -6 to -2
Outputs:
- audio_weight_grad: float32 [768, 512], replicated
- text_weight_grad: float32 [768, 512], replicated
All inputs are finite; a program needn't handle non-finite values.
Results may differ from a plain program's by a relative error of at most 0.0029.
Values may be sent and summed in bfloat16 or wider, within the bound.
A program may use at most 64 MiB of HBM per device.

v0:
```python
import jax
import jax.numpy as jnp
from jax import lax
from jax.sharding import PartitionSpec as P

EPSILON = 1e-06


def embed(features, weight):
    hidden = jnp.dot(features, weight, preferred_element_type=jnp.float32)
    norm_value = jnp.sqrt(jnp.sum(hidden * hidden, axis=1, keepdims=True) + EPSILON)
    return (hidden / norm_value, norm_value)


def unit_backward(grad, unit, norm_value):
    return (grad - unit * jnp.sum(unit * grad, axis=1, keepdims=True)) / norm_value


def weight_grad(features, hidden_grad):
    high_part = hidden_grad.astype(jnp.bfloat16)
    low_part = (hidden_grad - high_part.astype(jnp.float32)).astype(jnp.bfloat16)
    dims = (((0,), (0,)), ((), ()))
    first = lax.dot_general(features, high_part, dims, preferred_element_type=jnp.float32)
    second = lax.dot_general(features, low_part, dims, preferred_element_type=jnp.float32)
    return first + second


def per_device(audio_features, audio_weight, text_features, text_weight, logit_scale, logit_bias):
    row_count = audio_features.shape[0]
    group_size = lax.axis_size("group")
    cycle_size = lax.axis_size("blk")
    group_id = lax.axis_index("group")
    cycle_id = lax.axis_index("blk")
    temper = logit_scale[0]
    offset = logit_bias[0]
    own_clip_unit, own_clip_norm = embed(audio_features, audio_weight)
    own_text_unit, own_text_norm = embed(text_features, text_weight)
    clips = lax.all_gather(own_clip_unit.astype(jnp.bfloat16), "group", axis=0, tiled=True)
    texts = lax.all_gather(own_text_unit.astype(jnp.bfloat16), "blk", axis=0, tiled=True)
    clip_slot = jnp.arange(group_size * row_count, dtype=jnp.int32)
    clip_global = (
        cycle_id * group_size + clip_slot // row_count
    ) * row_count + clip_slot % row_count
    text_slot = jnp.arange(cycle_size * row_count, dtype=jnp.int32)
    text_global = (
        text_slot // row_count * group_size + group_id
    ) * row_count + text_slot % row_count
    logits = temper * jnp.dot(clips, texts.T, preferred_element_type=jnp.float32) + offset
    sign = jnp.where(clip_global[:, None] == text_global[None, :], 1.0, -1.0).astype(jnp.float32)
    gate = (-sign * jax.nn.sigmoid(-sign * logits)).astype(jnp.bfloat16)
    clip_terms = temper * jnp.dot(gate, texts, preferred_element_type=jnp.float32)
    product = lax.dot_general(
        gate, clips, (((0,), (0,)), ((), ())), preferred_element_type=jnp.float32
    )
    text_grad = lax.psum_scatter(temper * product, "blk", scatter_dimension=0, tiled=True)
    text_hidden_grad = unit_backward(text_grad, own_text_unit, own_text_norm)
    text_part = weight_grad(text_features, text_hidden_grad)
    clip_grad = lax.psum_scatter(clip_terms, "group", scatter_dimension=0, tiled=True)
    audio_hidden_grad = unit_backward(clip_grad, own_clip_unit, own_clip_norm)
    audio_part = weight_grad(audio_features, audio_hidden_grad)
    audio_total, text_total = lax.psum((audio_part, text_part), ("blk", "group"))
    return (audio_total, text_total)


def solution(mesh):
    placed = (P(("blk", "group"), None), P(), P(("blk", "group"), None), P(), P(), P())
    return jax.shard_map(
        per_device, mesh=mesh, in_specs=placed, out_specs=(P(), P()), check_vma=False
    )
```

profile of v0, /device:TPU:11, one launch (start us, length us, event | category | flops | bytes accessed | tf_op | source)
XLA Modules:
  0.0 300.9 jit_solution(6295735325619537805)
XLA Ops:
  7.2 0.0 copy-start
  7.2 0.0 all-gather.2.cloned.1.call-start
  7.2 1.1 copy-done
  8.3 1.3 multiply_reduce_fusion.2
  9.6 0.8 fusion.31
  10.4 0.0 all-gather.2.cloned.1.call-update
  10.4 0.0 reduce-scatter.3.cloned.1.call-start
  11.7 1.6 multiply_reduce_fusion.3
  13.3 0.1 fusion.30
  13.4 5.0 %all_gather.6 = bf16[256,512]{1,0:T(8,128)(2,1)S(1)} all-gather(bf16[128,512]{1,0:T(8,128)(2,1)S(1)} %fusion.30), channel_id=1, replica_groups=mesh['blk'=16,'group'=2] {'group'}, dimensions={0}, use_global_device_ids=true | all-gather | bytes 393216 | tf_op jit(solution)/shard_map/all_gather | solution.py:38
  18.5 33.4 %all-gather.2.cloned.1.call-done = bf16[2048,512]{1,0:T(8,128)(2,1)} async-done(((bf16[128,512]{1,0:T(8,128)(2,1)}), bf16[2048,512]{1,0:T(8,128)(2,1)}) %all-gather.2.cloned.1.call-update) | async-done | bytes 2097168 | tf_op jit(solution)/shard_map/all_gather | solution.py:39
  51.9 0.0 copy-start.6
  51.9 2.9 fusion.7
  54.8 0.0 copy-done.6
  54.8 1.5 convolution_multiply_fusion.2
  56.3 0.0 reduce-scatter.3.cloned.1.call-update
  56.3 0.0 reduce-scatter.5.cloned.1.call-start
  56.4 2.7 convolution_multiply_fusion
  59.1 0.0 copy-start.3
  59.1 0.0 reduce-scatter.5.cloned.1.call-update
  59.1 0.0 all-reduce.3.cloned.1.call-start
  59.1 12.1 %reduce-scatter.3.cloned.1.call-done = f32[128,512]{1,0:T(8,128)} async-done(((f32[256,512]{1,0:T(8,128)}), f32[128,512]{1,0:T(8,128)}) %reduce-scatter.3.cloned.1.call-update) | async-done | bytes 262160 | tf_op jit(solution)/shard_map/reduce_scatter | solution.py:58
  71.3 0.0 copy-start.1
  71.3 1.2 multiply_reduce_fusion.1
  72.5 0.0 copy-done.3
  72.5 1.4 fusion.12
  73.9 0.0 copy-done.1
  74.0 0.0 copy-start.4
  74.0 1.6 add_bitcast_fusion.1
  75.6 70.8 %reduce-scatter.5.cloned.1.call-done = f32[128,512]{1,0:T(8,128)} async-done(((f32[2048,512]{1,0:T(8,128)}), f32[128,512]{1,0:T(8,128)}) %reduce-scatter.5.cloned.1.call-update) | async-done | bytes 262160 | tf_op jit(solution)/shard_map/reduce_scatter | solution.py:55
  146.4 0.0 copy-start.2
  146.4 1.2 multiply_reduce_fusion
  147.6 0.0 copy-done.4
  147.6 1.4 fusion.9
  149.0 0.0 copy-done.2
  149.0 1.6 add_bitcast_fusion
  150.7 0.0 all-reduce.3.cloned.1.call-update
  150.7 138.9 %all-reduce.3.cloned.1.call-done = (f32[768,512]{0,1:T(8,128)}, f32[768,512]{0,1:T(8,128)}) async-done(((f32[768,512]{0,1:T(8,128)}, f32[768,512]{0,1:T(8,128)}), (f32[768,512]{0,1:T(8,128)}, f32[768,512]{0,1:T(8,128)})) %all-reduce.3.cloned.1.call-update) | async-done | bytes 3145744 | tf_op jit(solution)/shard_map/psum | solution.py:61
  289.6 0.0 copy-start.5
  289.6 3.1 %copy.8 = f32[768,512]{1,0:T(8,128)} copy(f32[768,512]{0,1:T(8,128)} %get-tuple-element.4) | data formatting | bytes 3145728
  292.7 0.0 copy-done.5
  292.7 1.6 copy.9
  (4 shorter events, 0.0 us)
Async XLA Ops:
  7.2 1.1 copy-start
  7.2 44.7 %all-gather.2.cloned.1.call-start = ((), (), s32[]{:S(2)}) async-start(), calls=%async_computation.2 | async-start | bytes 2228224 | tf_op jit(solution)/shard_map/all_gather | solution.py:39
  10.4 60.9 %reduce-scatter.3.cloned.1.call-start = ((), (), s32[]{:S(2)}) async-start(), calls=%async_computation.3 | async-start | bytes 786432 | tf_op jit(solution)/shard_map/reduce_scatter | solution.py:58
  51.9 2.9 copy-start.6
  56.3 90.0 %reduce-scatter.5.cloned.1.call-start = ((), (), s32[]{:S(2)}) async-start(), calls=%async_computation.4 | async-start | bytes 4456448 | tf_op jit(solution)/shard_map/reduce_scatter | solution.py:55
  59.1 13.4 %copy-start.3 = (bf16[128,768]{1,0:T(8,128)(2,1)S(1)}, bf16[128,768]{1,0:T(8,128)(2,1)}, u32[]{:S(2)}) copy-start(bf16[128,768]{1,0:T(8,128)(2,1)} %param.6) | copy-start | bytes 589828
  59.1 230.5 %all-reduce.3.cloned.1.call-start = ((), (), s32[]{:S(2)}) async-start(), calls=%async_computation.5 | async-start | bytes 6291456 | tf_op jit(solution)/shard_map/psum | solution.py:61
  71.3 2.7 copy-start.1
  74.0 73.6 %copy-start.4 = (bf16[128,768]{1,0:T(8,128)(2,1)S(1)}, bf16[128,768]{1,0:T(8,128)(2,1)}, u32[]{:S(2)}) copy-start(bf16[128,768]{1,0:T(8,128)(2,1)} %param.8) | copy-start | bytes 589828
  146.4 2.7 copy-start.2
  289.6 3.1 %copy-start.5 = (f32[768,512]{0,1:T(8,128)S(1)}, f32[768,512]{0,1:T(8,128)}, u32[]{:S(2)}) copy-start(f32[768,512]{0,1:T(8,128)} %get-tuple-element.5) | copy-start | bytes 4718596
Sparse Core Ops, SparseCore 0:
  10.7 41.0 all-gather.1
  56.5 14.7 reduce-scatter.2
  75.6 70.6 reduce-scatter.4
  152.5 137.1 all-reduce.2
where the time goes:
time: 305 us; the launch traced here: 301 us
  waiting for transfers between devices  255 us (84%)
  matrix products  16.1 us (5%)
  between operations  15.2 us (5%)
  local copies, waits for them, and re-layouts  5.86 us (2%)
  blocking collectives  5.04 us (2%)
  other arithmetic  3.3 us (1%)
    psum x1, waiting for transfers between devices, per_device(): lax.psum((audio_part, text_part), ('blk', 'group'))  139 us
    reduce_scatter x1, waiting for transfers between devices, per_device(): lax.psum_scatter(temper * product, 'blk', scatter_dimension=0, tiled=True)  70.8 us
    all_gather x1, waiting for transfers between devices, per_device(): lax.all_gather(own_text_unit.astype(jnp.bfloat16), 'blk', axis=0, tiled=T...  33.4 us
    reduce_scatter x1, waiting for transfers between devices, per_device(): lax.psum_scatter(clip_terms, 'group', scatter_dimension=0, tiled=True)  12.1 us
  transfers between devices with their start and end apart: 4, of which 4 were waited for; matrix products, arithmetic and copies ran while one was open for 3% of the time, Pallas kernels for 0%

commit v1 on v0

v1 whole, which is shorter than its diff:
```python
import functools

import jax
import jax.numpy as jnp
from jax import lax
from jax.experimental import pallas as pl
from jax.experimental.pallas import tpu as pltpu
from jax.sharding import PartitionSpec as P

EPSILON = 1e-06
BF16 = jnp.bfloat16
F32 = jnp.float32
INNER = 4
TN = (((0,), (0,)), ((), ()))
NT = (((1,), (1,)), ((), ()))


def kernel(
    blocks, groups,
    audio_ref, audio_w_ref, text_ref, text_w_ref, scale_ref, bias_ref,
    out_ref,
    clips, texts, staged, feats, gates, clip_send, clip_recv, text_send, text_recv,
    clip_own, text_own, units, norms, hid_send, hid_recv, partial, part_recv,
    s_clip, r_clip, s_text, r_text, s_feat, r_feat, s_cg, r_cg, s_tg, r_tg,
    s_hid, r_hid, s_part, r_part, s_agz, r_agz, s_agp, r_agp, s_agc, r_agc,
):
    depth = blocks // INNER
    plane = INNER * groups
    rows = audio_ref.shape[0]
    width = audio_w_ref.shape[1]
    lanes = width // 4
    span = audio_w_ref.shape[0] // depth
    blk = lax.axis_index("blk")
    group = lax.axis_index("group")
    zed = lax.div(blk, INNER)
    inner = lax.rem(blk, INNER)
    me = inner * groups + group

    def at_plane(a):
        return (zed * INNER + lax.div(a, groups), lax.rem(a, groups))

    def at_depth(z):
        return (z * INNER + inner, group)

    def role(a):
        i, g = lax.div(a, groups), lax.rem(a, groups)
        return lax.rem(i, 2) * 4 + lax.div(i, 2) * 2 + lax.rem(g, 2)

    def copy(src, dst, send, recv, device):
        return pltpu.make_async_remote_copy(
            src_ref=src, dst_ref=dst, send_sem=send, recv_sem=recv,
            device_id=device, device_id_type=pl.DeviceIdType.MESH,
        )

    def peers(count, own, fn):
        def body(k, carry):
            fn(lax.rem(own + k, count))
            return carry
        lax.fori_loop(1, count, body, 0)

    mine = role(me)
    kind = lax.div(mine, 4)
    part = lax.rem(mine, 4)

    barrier = pltpu.get_barrier_semaphore()
    peers(plane, me, lambda a: pl.semaphore_signal(
        barrier, inc=1, device_id=at_plane(a), device_id_type=pl.DeviceIdType.MESH))
    peers(depth, zed, lambda z: pl.semaphore_signal(
        barrier, inc=1, device_id=at_depth(z), device_id_type=pl.DeviceIdType.MESH))

    def embed(at, features, weight):
        hidden = jnp.dot(features[...], weight[...], preferred_element_type=F32)
        norm = jnp.sqrt(jnp.sum(hidden * hidden, axis=1, keepdims=True) + EPSILON)
        unit = hidden / norm
        units[at] = unit
        norms[at] = jnp.broadcast_to(norm, (rows, 128))
        return unit.astype(BF16)

    texts[zed] = embed(1, text_ref, text_w_ref)
    pl.semaphore_wait(barrier, plane - 1 + depth - 1)

    def send_text(z):
        copy(texts.at[zed], texts.at[zed], s_text.at[z], r_text.at[zed], at_depth(z)).start()
    peers(depth, zed, send_text)

    clips[me] = embed(0, audio_ref, audio_w_ref)

    def send_clip(a):
        copy(clips.at[me], clips.at[me], s_clip.at[a], r_clip.at[me], at_plane(a)).start()
    peers(plane, me, send_clip)

    staged[0] = audio_ref[...]
    staged[1] = text_ref[...]
    feats[me] = staged[kind]

    def got(buf, at, recv, send):
        copy(buf.at[at], buf.at[at], send.at[at], recv.at[at], (blk, group)).wait_recv()

    peers(depth, zed, lambda z: got(texts, z, r_text, s_text))

    scale = scale_ref[0]
    bias = bias_ref[0]
    all_texts = lambda: texts[...].reshape(depth * rows, width)

    def gate_block(a, own):
        logits = scale * lax.dot_general(clips[a], all_texts(), NT, preferred_element_type=F32) + bias
        if own:
            row = lax.broadcasted_iota(jnp.int32, logits.shape, 0)
            column = lax.broadcasted_iota(jnp.int32, logits.shape, 1)
            sign = jnp.where(column - row == zed * rows, 1.0, -1.0)
            gate = (-sign / (1.0 + jnp.exp(sign * logits))).astype(BF16)
        else:
            gate = (1.0 / (1.0 + jnp.exp(-logits))).astype(BF16)
        gates[a] = gate
        return jnp.dot(gate, all_texts(), preferred_element_type=F32)

    clip_own[...] = gate_block(me, True)

    def clip_step(a):
        got(clips, a, r_clip, s_clip)
        clip_send[a] = gate_block(a, False).astype(BF16)
        copy(clip_send.at[a], clip_recv.at[me], s_cg.at[a], r_cg.at[me], at_plane(a)).start()
    peers(plane, me, clip_step)

    def text_term(z):
        start = pl.multiple_of(z * rows, rows)
        block = gates[:, :, pl.ds(start, rows)].reshape(plane * rows, rows)
        return lax.dot_general(
            block, clips[...].reshape(plane * rows, width), TN, preferred_element_type=F32)

    def text_step(z):
        text_send[z] = text_term(z).astype(BF16)
        copy(text_send.at[z], text_recv.at[zed], s_tg.at[z], r_tg.at[zed], at_depth(z)).start()
    peers(depth, zed, text_step)

    def send_feat(a):
        copy(staged.at[lax.div(role(a), 4)], feats.at[me], s_feat.at[a], r_feat.at[me], at_plane(a)).start()
    peers(plane, me, send_feat)

    text_own[...] = text_term(zed)

    def backward(at, own, grad):
        unit = units[at]
        grad = scale * grad
        inner_sum = jnp.sum(unit * grad, axis=1, keepdims=True)
        result = (grad - unit * inner_sum) / norms[at][:, :1]
        for s in range(4):
            hid_send[4 * at + s] = result[:, s * lanes:(s + 1) * lanes]

    def add_clip(a):
        got(clip_recv, a, r_cg, s_cg)
        clip_own[...] += clip_recv[a].astype(F32)
    peers(plane, me, add_clip)
    backward(0, clip_own, clip_own[...])

    def send_hid(want, a):
        @pl.when(lax.div(role(a), 4) == want)
        def _():
            copy(hid_send.at[role(a)], hid_recv.at[me], s_hid.at[a], r_hid.at[me], at_plane(a)).start()
    peers(plane, me, functools.partial(send_hid, 0))

    def add_text(z):
        got(text_recv, z, r_tg, s_tg)
        text_own[...] += text_recv[z].astype(F32)
    peers(depth, zed, add_text)
    backward(1, text_own, text_own[...])
    peers(plane, me, functools.partial(send_hid, 1))
    hid_recv[me] = hid_send[mine]

    peers(plane, me, lambda a: got(feats, a, r_feat, s_feat))
    peers(plane, me, lambda a: got(hid_recv, a, r_hid, s_hid))
    hidden = hid_recv[...].reshape(plane * rows, lanes)
    high = hidden.astype(BF16)
    low = (hidden - high.astype(F32)).astype(BF16)
    both = lax.dot_general(
        feats[...].reshape(plane * rows, feats.shape[2]),
        jnp.concatenate([high, low], axis=1), TN, preferred_element_type=F32)
    partial[...] = (both[:, :lanes] + both[:, lanes:]).reshape(partial.shape)

    def send_part(z):
        copy(partial.at[z], part_recv.at[zed], s_part.at[z], r_part.at[zed], at_depth(z)).start()
    peers(depth, zed, send_part)
    part_recv[zed] = partial[zed]
    peers(depth, zed, lambda z: got(part_recv, z, r_part, s_part))
    total = part_recv[0]
    for z in range(1, depth):
        total = total + part_recv[z]

    def piece(k, p, z):
        return out_ref.at[k, p, pl.ds(pl.multiple_of(z * span, span), span)]

    out_ref[kind, part, pl.ds(pl.multiple_of(zed * span, span), span)] = total.astype(BF16)

    near = lax.div(group, 2) * 2
    sibling = (zed * INNER + inner + 1 - 2 * kind, group)

    def same_core(p):
        return (zed * INNER + lax.div(p, 2) * 2 + kind, near + lax.rem(p, 2))

    def send_z(z):
        copy(piece(kind, part, zed), piece(kind, part, zed), s_agz.at[z], r_agz.at[zed], at_depth(z)).start()
    peers(depth, zed, send_z)

    def to_sibling(p, z):
        here = piece(kind, p, z)
        copy(here, here, s_agc.at[p, z], r_agc.at[p, z], sibling).start()

    def spread(z):
        here = piece(kind, part, z)

        def send(p):
            copy(here, here, s_agp.at[p, z], r_agp.at[part, z], same_core(p)).start()
        peers(4, part, send)
        to_sibling(part, z)

    spread(zed)

    def take_z(z):
        here = piece(kind, part, z)
        copy(here, here, s_agz.at[z], r_agz.at[z], (blk, group)).wait_recv()
        spread(z)
    peers(depth, zed, take_z)

    def relay(k, carry):
        z = lax.rem(zed + k, depth)

        def take(p):
            here = piece(kind, p, z)
            copy(here, here, s_agp.at[p, z], r_agp.at[p, z], (blk, group)).wait_recv()
            to_sibling(p, z)
        peers(4, part, take)
        return carry
    lax.fori_loop(0, depth, relay, 0)

    def finish(k, carry):
        z = lax.rem(zed + k, depth)
        for p in range(4):
            there = piece(1 - kind, p, z)
            copy(there, there, s_agc.at[p, z], r_agc.at[p, z], sibling).wait_recv()
        return carry
    lax.fori_loop(0, depth, finish, 0)

    def sent(src, send, recv, at):
        copy(src, src, send.at[at], recv.at[at], (blk, group)).wait_send()

    def drain_plane(a):
        sent(clips.at[me], s_clip, r_clip, a)
        sent(staged.at[0], s_feat, r_feat, a)
        sent(clip_send.at[a], s_cg, r_cg, a)
        sent(hid_send.at[0], s_hid, r_hid, a)
    peers(plane, me, drain_plane)

    def drain_depth(z):
        sent(texts.at[zed], s_text, r_text, z)
        sent(text_send.at[z], s_tg, r_tg, z)
        sent(partial.at[z], s_part, r_part, z)
        sent(piece(kind, part, zed), s_agz, r_agz, z)
    peers(depth, zed, drain_depth)

    def drain_out(z, carry):
        def one(p):
            here = piece(kind, part, z)
            copy(here, here, s_agp.at[p, z], r_agp.at[p, z], (blk, group)).wait_send()
        peers(4, part, one)
        for p in range(4):
            here = piece(kind, p, z)
            copy(here, here, s_agc.at[p, z], r_agc.at[p, z], sibling).wait_send()
        return carry
    lax.fori_loop(0, depth, drain_out, 0)


def per_device(blocks, groups, audio, audio_w, text, text_w, scale, bias):
    rows, wide = audio.shape
    width = audio_w.shape[1]
    depth, plane = blocks // INNER, INNER * groups
    lanes, span = width // 4, wide // depth
    vmem = pl.BlockSpec(memory_space=pltpu.VMEM)
    smem = pl.BlockSpec(memory_space=pltpu.SMEM)
    dma = pltpu.SemaphoreType.DMA
    sems = []
    for count in (plane, depth, plane, plane, depth, plane, depth, depth):
        sems += [dma((count,)), dma((count,))]
    sems += [dma((4, depth))] * 4
    out = pl.pallas_call(
        functools.partial(kernel, blocks, groups),
        out_shape=jax.ShapeDtypeStruct((2, 4, wide, lanes), BF16),
        in_specs=[vmem, vmem, vmem, vmem, smem, smem],
        out_specs=vmem,
        scratch_shapes=[
            pltpu.VMEM((plane, rows, width), BF16),
            pltpu.VMEM((depth, rows, width), BF16),
            pltpu.VMEM((2, rows, wide), BF16),
            pltpu.VMEM((plane, rows, wide), BF16),
            pltpu.VMEM((plane, rows, depth * rows), BF16),
            pltpu.VMEM((plane, rows, width), BF16),
            pltpu.VMEM((plane, rows, width), BF16),
            pltpu.VMEM((depth, rows, width), BF16),
            pltpu.VMEM((depth, rows, width), BF16),
            pltpu.VMEM((rows, width), F32),
            pltpu.VMEM((rows, width), F32),
            pltpu.VMEM((2, rows, width), F32),
            pltpu.VMEM((2, rows, 128), F32),
            pltpu.VMEM((8, rows, lanes), F32),
            pltpu.VMEM((plane, rows, lanes), F32),
            pltpu.VMEM((depth, span, lanes), F32),
            pltpu.VMEM((depth, span, lanes), F32),
        ] + sems,
        compiler_params=pltpu.CompilerParams(
            collective_id=0, has_side_effects=True, vmem_limit_bytes=56 * 1024 * 1024),
    )(audio, audio_w, text, text_w, scale, bias)
    whole = out.astype(F32).transpose(0, 2, 1, 3).reshape(2, wide, width)
    return whole[0], whole[1]


def solution(mesh):
    placed = (P(("blk", "group"), None), P(), P(("blk", "group"), None), P(), P(), P())
    step = functools.partial(per_device, mesh.shape["blk"], mesh.shape["group"])
    return jax.shard_map(step, mesh=mesh, in_specs=placed, out_specs=(P(), P()), check_vma=False)
```

time: 305 us -> 93.1 us (0.31)
  the two profiles are of different devices: /device:TPU:11 before, /device:TPU:17 now
where the time goes in v1:
time: 93.1 us; the launch traced here: 92.9 us
  Pallas kernels  82.4 us (89%)
  local copies, waits for them, and re-layouts  6.91 us (7%)
  between operations  1.96 us (2%)
  other arithmetic  1.61 us (2%)
    pallas_call x1, Pallas kernels, per_device(): pl.pallas_call(functools.partial(kernel, blocks, groups), out_shape=jax.S...  82.4 us
    slice x3, local copies, waits for them, and re-layouts, per_device(): return (whole[0], whole[1])  3.68 us
    unnamed x2, local copies, waits for them, and re-layouts  3.23 us

profile of v1, /device:TPU:17, one launch (start us, length us, event | category | flops | bytes accessed | tf_op | source)
XLA Modules:
  0.0 92.9 jit_solution(687110677096447812)
XLA Ops:
  1.9 82.4 %shard_map.77 = bf16[2,4,768,128]{3,2,1,0:T(8,128)(2,1)} custom-call(bf16[128,768]{1,0:T(8,128)(2,1)} %audio_ref.1, bf16[768,512]{1,0:T(8,128)(2,1)} %audio_w_ref.1, bf16[128,768]{1,0:T(8,128)(2,1)} %text_ref.1, bf16[768,512]{1,0:T(8,128)(2,1)} %text_w_ref.1, f32[1]{0:T(128)S(6)} %copy.12.scale_ref, f32[1]{0:T(128)S(6)} %copy.13.bias_ref), custom_call_target="tpu_custom_call" | custom-call | tf_op jit(solution)/shard_map/pallas_call | solution.py:284
  84.4 1.6 %convert_bitcast_fusion = f32[2,768,4,128]{3,1,2,0:T(8,128)S(1)} fusion(bf16[2,4,768,128]{3,2,1,0:T(8,128)(2,1)} %shard_map.77), kind=kLoop, calls=%fused_computation | loop fusion | flops 786432 | bytes 4718592 | tf_op jit(solution)/shard_map/transpose | solution.py:311
  86.0 1.3 %fusion = (f32[1,768,4,128]{3,1,2,0:T(8,128)}, f32[1,768,4,128]{3,1,2,0:T(8,128)S(1)}) fusion(f32[2,768,4,128]{3,1,2,0:T(8,128)S(1)} %convert_bitcast_fusion), kind=kLoop, calls=%fused_computation.1 | loop fusion | bytes 6291456 | tf_op jit(solution)/shard_map/slice | solution.py:312
  87.3 1.9 %copy.9 = f32[1,768,4,128]{1,3,2,0:T(8,128)S(1)} copy(f32[1,768,4,128]{3,1,2,0:T(8,128)} %get-tuple-element.4) | data formatting | bytes 3145728 | tf_op jit(solution)/shard_map/slice | solution.py:312
  89.2 1.6 %copy.11 = f32[768,512]{1,0:T(8,128)} copy(f32[768,512]{0,1:T(8,128)S(1)} %bitcast.4) | data formatting | bytes 3145728
  90.8 0.5 copy.8
  91.3 1.6 %copy.10 = f32[768,512]{1,0:T(8,128)} copy(f32[768,512]{0,1:T(8,128)S(1)} %bitcast.5) | data formatting | bytes 3145728

commit v2 on v1

v2 whole, which is shorter than its diff:
```python
import functools

import jax
import jax.numpy as jnp
from jax import lax
from jax.experimental import pallas as pl
from jax.experimental.pallas import tpu as pltpu
from jax.sharding import PartitionSpec as P

EPSILON = 1e-06
BF16 = jnp.bfloat16
F32 = jnp.float32
INNER = 4
TN = (((0,), (0,)), ((), ()))
NT = (((1,), (1,)), ((), ()))


def kernel(
    blocks, groups,
    audio_ref, audio_w_ref, text_ref, text_w_ref, scale_ref, bias_ref,
    audio_out, text_out,
    clips, texts, staged, weights, feats, gates, clip_send, clip_recv, text_send, text_recv,
    clip_own, text_own, units, norms, hid_send, hid_recv, part_own, part_send, part_recv, gathered,
    s_in, s_clip, s_clipf, r_clip, s_text, r_text, s_feat, s_featf, r_feat, s_cg, r_cg, s_tg, r_tg,
    s_hid, r_hid, s_part, r_part, s_agz, r_agz, s_agp, r_agp, s_agc, r_agc,
):
    depth = blocks // INNER
    plane = INNER * groups
    rows = audio_ref.shape[0]
    width = audio_w_ref.shape[1]
    lanes = width // 4
    span = audio_w_ref.shape[0] // depth
    blk = lax.axis_index("blk")
    group = lax.axis_index("group")
    zed = lax.div(blk, INNER)
    inner = lax.rem(blk, INNER)
    me = inner * groups + group

    def at_plane(a):
        return (zed * INNER + lax.div(a, groups), lax.rem(a, groups))

    def at_depth(z):
        return (z * INNER + inner, group)

    half = plane // 2
    core = lax.rem(inner, 2)
    pos = lax.div(inner, 2) * groups + group
    sibling = (zed * INNER + inner + 1 - 2 * core, group)

    def block_at(q, c):
        return (lax.div(q, groups) * 2 + c) * groups + lax.rem(q, groups)

    def kind_of(a):
        return lax.rem(lax.rem(a, groups), 2)

    def role(a):
        return kind_of(a) * 4 + lax.div(a, groups)

    sources = (audio_ref, text_ref, audio_w_ref, text_w_ref)
    targets = (staged.at[0], staged.at[1], weights.at[0], weights.at[1])
    loads = [pltpu.make_async_copy(sources[k], targets[k], s_in.at[k]) for k in range(4)]
    for k in (1, 3, 0, 2):
        loads[k].start()

    def copy(src, dst, send, recv, device):
        return pltpu.make_async_remote_copy(
            src_ref=src, dst_ref=dst, send_sem=send, recv_sem=recv,
            device_id=device, device_id_type=pl.DeviceIdType.MESH,
        )

    def peers(count, own, fn):
        def body(k, carry):
            fn(lax.rem(own + k, count))
            return carry
        lax.fori_loop(1, count, body, 0)

    mine = role(me)
    kind = kind_of(me)

    barrier = pltpu.get_barrier_semaphore()
    peers(plane, me, lambda a: pl.semaphore_signal(
        barrier, inc=1, device_id=at_plane(a), device_id_type=pl.DeviceIdType.MESH))
    peers(depth, zed, lambda z: pl.semaphore_signal(
        barrier, inc=1, device_id=at_depth(z), device_id_type=pl.DeviceIdType.MESH))

    def embed(at):
        hidden = jnp.dot(staged[at], weights[at], preferred_element_type=F32)
        norm = jnp.sqrt(jnp.sum(hidden * hidden, axis=1, keepdims=True) + EPSILON)
        unit = hidden / norm
        units[at] = unit
        norms[at] = jnp.broadcast_to(norm, (rows, 128))
        return unit.astype(BF16)

    loads[1].wait()
    loads[3].wait()
    texts[zed] = embed(1)
    pl.semaphore_wait(barrier, plane - 1 + depth - 1)

    def send_text(z):
        copy(texts.at[zed], texts.at[zed], s_text.at[z], r_text.at[zed], at_depth(z)).start()
    peers(depth, zed, send_text)

    loads[0].wait()
    loads[2].wait()
    clips[me] = embed(0)

    def send_clip(q):
        copy(clips.at[me], clips.at[me], s_clip.at[q], r_clip.at[me], at_plane(block_at(q, core))).start()
    peers(half, pos, send_clip)
    copy(clips.at[me], clips.at[me], s_clipf.at[pos], r_clip.at[me], sibling).start()

    feats[me] = staged[kind]

    def send_feat(q):
        a = block_at(q, core)
        copy(staged.at[kind_of(a)], feats.at[me], s_feat.at[q], r_feat.at[me], at_plane(a)).start()
    peers(half, pos, send_feat)
    copy(staged.at[kind], feats.at[me], s_featf.at[pos], r_feat.at[me], sibling).start()

    def got(buf, at, recv, send):
        copy(buf.at[at], buf.at[at], send.at[0], recv.at[at], (blk, group)).wait_recv()

    def pass_clip(q):
        a = block_at(q, core)
        got(clips, a, r_clip, s_clip)
        copy(clips.at[a], clips.at[a], s_clipf.at[q], r_clip.at[a], sibling).start()
    peers(half, pos, pass_clip)

    peers(depth, zed, lambda z: got(texts, z, r_text, s_text))

    scale = scale_ref[0]
    bias = bias_ref[0]
    all_texts = lambda: texts[...].reshape(depth * rows, width)

    def gate_block(a, own):
        logits = scale * lax.dot_general(clips[a], all_texts(), NT, preferred_element_type=F32) + bias
        if own:
            row = lax.broadcasted_iota(jnp.int32, logits.shape, 0)
            column = lax.broadcasted_iota(jnp.int32, logits.shape, 1)
            sign = jnp.where(column - row == zed * rows, 1.0, -1.0)
            gate = (-sign / (1.0 + jnp.exp(sign * logits))).astype(BF16)
        else:
            gate = (1.0 / (1.0 + jnp.exp(-logits))).astype(BF16)
        gates[a] = gate
        return jnp.dot(gate, all_texts(), preferred_element_type=F32)

    clip_own[...] = gate_block(me, True)

    def clip_step(a):
        clip_send[a] = gate_block(a, False).astype(BF16)
        copy(clip_send.at[a], clip_recv.at[me], s_cg.at[a], r_cg.at[me], at_plane(a)).start()
    peers(half, pos, lambda q: clip_step(block_at(q, core)))

    def clip_other(q, carry):
        a = block_at(q, 1 - core)
        got(clips, a, r_clip, s_clip)
        clip_step(a)
        return carry
    lax.fori_loop(0, half, clip_other, 0)

    def text_term(z):
        start = pl.multiple_of(z * rows, rows)
        block = gates[:, :, pl.ds(start, rows)].reshape(plane * rows, rows)
        return lax.dot_general(
            block, clips[...].reshape(plane * rows, width), TN, preferred_element_type=F32)

    def text_step(z):
        text_send[z] = text_term(z).astype(BF16)
        copy(text_send.at[z], text_recv.at[zed], s_tg.at[z], r_tg.at[zed], at_depth(z)).start()
    peers(depth, zed, text_step)

    def pass_feat(q):
        a = block_at(q, core)
        got(feats, a, r_feat, s_feat)
        copy(feats.at[a], feats.at[a], s_featf.at[q], r_feat.at[a], sibling).start()
    peers(half, pos, pass_feat)

    text_own[...] = text_term(zed)

    def backward(at, own, grad):
        unit = units[at]
        grad = scale * grad
        inner_sum = jnp.sum(unit * grad, axis=1, keepdims=True)
        result = (grad - unit * inner_sum) / norms[at][:, :1]
        for s in range(4):
            hid_send[4 * at + s] = result[:, s * lanes:(s + 1) * lanes]

    def add_clip(a):
        got(clip_recv, a, r_cg, s_cg)
        clip_own[...] += clip_recv[a].astype(F32)
    peers(plane, me, add_clip)
    backward(0, clip_own, clip_own[...])

    def send_hid(want, a):
        @pl.when(kind_of(a) == want)
        def _():
            copy(hid_send.at[role(a)], hid_recv.at[me], s_hid.at[a], r_hid.at[me], at_plane(a)).start()
    peers(plane, me, functools.partial(send_hid, 0))

    def add_text(z):
        got(text_recv, z, r_tg, s_tg)
        text_own[...] += text_recv[z].astype(F32)
    peers(depth, zed, add_text)
    backward(1, text_own, text_own[...])
    peers(plane, me, functools.partial(send_hid, 1))
    hid_recv[me] = hid_send[mine]

    def take_feat(q, carry):
        got(feats, block_at(q, 1 - core), r_feat, s_feat)
        return carry
    lax.fori_loop(0, half, take_feat, 0)
    peers(plane, me, lambda a: got(hid_recv, a, r_hid, s_hid))
    hidden = hid_recv[...].reshape(plane * rows, lanes)
    high = hidden.astype(BF16)
    low = (hidden - high.astype(F32)).astype(BF16)
    both = lax.dot_general(
        feats[...].reshape(plane * rows, feats.shape[2]),
        jnp.concatenate([high, low], axis=1), TN, preferred_element_type=F32)
    terms = (both[:, :lanes] + both[:, lanes:]).reshape(part_own.shape)
    part_own[...] = terms
    part_send[...] = terms.astype(BF16)

    def send_part(z):
        copy(part_send.at[z], part_recv.at[zed], s_part.at[z], r_part.at[zed], at_depth(z)).start()
    peers(depth, zed, send_part)
    part_recv[zed] = jnp.zeros(part_recv.shape[1:], BF16)
    peers(depth, zed, lambda z: got(part_recv, z, r_part, s_part))
    total = part_own[zed]
    for z in range(depth):
        total = total + part_recv[z].astype(F32)

    def piece(q, c, z):
        return gathered.at[lax.div(q, 2), lax.rem(q, 2) * 2 + c, pl.ds(pl.multiple_of(z * span, span), span)]

    own = kind * 2 + lax.div(inner, 2)
    near = lax.div(group, 2) * 2
    gathered[kind, inner, pl.ds(pl.multiple_of(zed * span, span), span)] = total.astype(BF16)

    def same_core(q):
        return (zed * INNER + lax.rem(q, 2) * 2 + core, near + lax.div(q, 2))

    def send_z(z):
        here = piece(own, core, zed)
        copy(here, here, s_agz.at[z], r_agz.at[zed], at_depth(z)).start()
    peers(depth, zed, send_z)

    def to_sibling(q, z):
        here = piece(q, core, z)
        copy(here, here, s_agc.at[q, z], r_agc.at[q, z], sibling).start()

    def spread(z):
        here = piece(own, core, z)

        def send(q):
            copy(here, here, s_agp.at[q, z], r_agp.at[own, z], same_core(q)).start()
        peers(4, own, send)
        to_sibling(own, z)

    spread(zed)

    def take_z(z):
        here = piece(own, core, z)
        copy(here, here, s_agz.at[z], r_agz.at[z], (blk, group)).wait_recv()
        spread(z)
    peers(depth, zed, take_z)

    def relay(k, carry):
        z = lax.rem(zed + k, depth)

        def take(q):
            here = piece(q, core, z)
            copy(here, here, s_agp.at[q, z], r_agp.at[q, z], (blk, group)).wait_recv()
            to_sibling(q, z)
        peers(4, own, take)
        return carry
    lax.fori_loop(0, depth, relay, 0)

    def finish(k, carry):
        z = lax.rem(zed + k, depth)
        for q in range(4):
            there = piece(q, 1 - core, z)
            copy(there, there, s_agc.at[q, z], r_agc.at[q, z], sibling).wait_recv()
        return carry
    lax.fori_loop(0, depth, finish, 0)
    for p in range(4):
        audio_out[:, p * lanes:(p + 1) * lanes] = gathered[0, p]
        text_out[:, p * lanes:(p + 1) * lanes] = gathered[1, p]

    def sent(src, send, recv, at):
        copy(src, src, send.at[at], recv.at[at], (blk, group)).wait_send()

    def drain_half(q, carry):
        sent(clips.at[me], s_clipf, r_clip, q)
        sent(staged.at[0], s_featf, r_feat, q)
        return carry
    lax.fori_loop(0, half, drain_half, 0)

    def drain_same(q):
        sent(clips.at[me], s_clip, r_clip, q)
        sent(staged.at[0], s_feat, r_feat, q)
    peers(half, pos, drain_same)

    def drain_plane(a):
        sent(clip_send.at[a], s_cg, r_cg, a)
        sent(hid_send.at[0], s_hid, r_hid, a)
    peers(plane, me, drain_plane)

    def drain_depth(z):
        sent(texts.at[zed], s_text, r_text, z)
        sent(text_send.at[z], s_tg, r_tg, z)
        sent(part_send.at[z], s_part, r_part, z)
        sent(piece(own, core, zed), s_agz, r_agz, z)
    peers(depth, zed, drain_depth)

    def drain_out(z, carry):
        def one(q):
            here = piece(own, core, z)
            copy(here, here, s_agp.at[q, z], r_agp.at[q, z], (blk, group)).wait_send()
        peers(4, own, one)
        for q in range(4):
            here = piece(q, core, z)
            copy(here, here, s_agc.at[q, z], r_agc.at[q, z], sibling).wait_send()
        return carry
    lax.fori_loop(0, depth, drain_out, 0)


def per_device(blocks, groups, audio, audio_w, text, text_w, scale, bias):
    rows, wide = audio.shape
    width = audio_w.shape[1]
    depth, plane = blocks // INNER, INNER * groups
    lanes, span = width // 4, wide // depth
    vmem = pl.BlockSpec(memory_space=pltpu.VMEM)
    smem = pl.BlockSpec(memory_space=pltpu.SMEM)
    dma = pltpu.SemaphoreType.DMA
    half = plane // 2
    sems = [dma((count,)) for count in (
        4, half, half, plane, depth, depth, half, half, plane, plane, plane, depth, depth,
        plane, plane, depth, depth, depth, depth)]
    sems += [dma((4, depth))] * 4
    whole = jax.ShapeDtypeStruct((wide, width), BF16)
    hbm = pl.BlockSpec(memory_space=pl.ANY)
    grads = pl.pallas_call(
        functools.partial(kernel, blocks, groups),
        out_shape=(whole, whole),
        in_specs=[hbm, hbm, hbm, hbm, smem, smem],
        out_specs=(vmem, vmem),
        scratch_shapes=[
            pltpu.VMEM((plane, rows, width), BF16),
            pltpu.VMEM((depth, rows, width), BF16),
            pltpu.VMEM((2, rows, wide), BF16),
            pltpu.VMEM((2, wide, width), BF16),
            pltpu.VMEM((plane, rows, wide), BF16),
            pltpu.VMEM((plane, rows, depth * rows), BF16),
            pltpu.VMEM((plane, rows, width), BF16),
            pltpu.VMEM((plane, rows, width), BF16),
            pltpu.VMEM((depth, rows, width), BF16),
            pltpu.VMEM((depth, rows, width), BF16),
            pltpu.VMEM((rows, width), F32),
            pltpu.VMEM((rows, width), F32),
            pltpu.VMEM((2, rows, width), F32),
            pltpu.VMEM((2, rows, 128), F32),
            pltpu.VMEM((8, rows, lanes), F32),
            pltpu.VMEM((plane, rows, lanes), F32),
            pltpu.VMEM((depth, span, lanes), F32),
            pltpu.VMEM((depth, span, lanes), BF16),
            pltpu.VMEM((depth, span, lanes), BF16),
            pltpu.VMEM((2, 4, wide, lanes), BF16),
        ] + sems,
        compiler_params=pltpu.CompilerParams(
            collective_id=0, has_side_effects=True, vmem_limit_bytes=56 * 1024 * 1024),
    )(audio, audio_w, text, text_w, scale, bias)
    return tuple(grad.astype(F32) for grad in grads)


def solution(mesh):
    placed = (P(("blk", "group"), None), P(), P(("blk", "group"), None), P(), P(), P())
    step = functools.partial(per_device, mesh.shape["blk"], mesh.shape["group"])
    return jax.shard_map(step, mesh=mesh, in_specs=placed, out_specs=(P(), P()), check_vma=False)
```

time: 93.1 us -> 71.5 us (0.77)
  the two profiles are of different devices: /device:TPU:17 before, /device:TPU:11 now
where the time goes in v2:
time: 71.5 us; the launch traced here: 71.4 us
  Pallas kernels  65.5 us (92%)
  other arithmetic  3.92 us (5%)
  between operations  1.94 us (3%)
    pallas_call x1, Pallas kernels, per_device(): pl.pallas_call(functools.partial(kernel, blocks, groups), out_shape=(whol...  65.5 us
    convert_element_type x2, other arithmetic, per_device(): return tuple((grad.astype(F32) for grad in grads))  3.92 us

profile of v2, /device:TPU:11, one launch (start us, length us, event | category | flops | bytes accessed | tf_op | source)
XLA Modules:
  0.0 71.4 jit_solution(6765019909801574219)
XLA Ops:
  1.9 65.5 %shard_map.77 = (bf16[768,512]{1,0:T(8,128)(2,1)}, bf16[768,512]{1,0:T(8,128)(2,1)}) custom-call(bf16[128,768]{1,0:T(8,128)(2,1)} %audio_ref.1, bf16[768,512]{1,0:T(8,128)(2,1)} %audio_w_ref.1, bf16[128,768]{1,0:T(8,128)(2,1)} %text_ref.1, bf16[768,512]{1,0:T(8,128)(2,1)} %text_w_ref.1, f32[1]{0:T(128)S(6)} %copy.8.scale_ref, f32[1]{0:T(128)S(6)} %copy.9.bias_ref), custom_call_target="tpu_custom_call" | custom-call | tf_op jit(solution)/shard_map/pallas_call | solution.py:342
  67.4 0.0 copy-start
  67.4 2.6 %convert_element_type.6 = f32[768,512]{1,0:T(8,128)} convert(bf16[768,512]{1,0:T(8,128)(2,1)} %get-tuple-element.4) | non-fusion elementwise | flops 393216 | bytes 2359296 | tf_op jit(solution)/shard_map/convert_element_type | solution.py:372
  70.0 0.0 copy-done
  70.0 1.4 %convert_element_type.7 = f32[768,512]{1,0:T(8,128)} convert(bf16[768,512]{1,0:T(8,128)(2,1)S(1)} %copy-done) | non-fusion elementwise | flops 393216 | bytes 2359296 | tf_op jit(solution)/shard_map/convert_element_type | solution.py:372
Async XLA Ops:
  67.4 2.6 %copy-start = (bf16[768,512]{1,0:T(8,128)(2,1)S(1)}, bf16[768,512]{1,0:T(8,128)(2,1)}, u32[]{:S(2)}) copy-start(bf16[768,512]{1,0:T(8,128)(2,1)} %get-tuple-element.5) | copy-start | bytes 2359300

commit v3 on v2

--- a/solution.py
+++ b/solution.py
@@ -19,9 +19,9 @@
     blocks, groups,
     audio_ref, audio_w_ref, text_ref, text_w_ref, scale_ref, bias_ref,
     audio_out, text_out,
-    clips, texts, staged, weights, feats, gates, clip_send, clip_recv, text_send, text_recv,
+    clips, texts, staged, weights, feats, gates, clip_give, clip_take, clip_send, clip_recv, text_send, text_recv,
     clip_own, text_own, units, norms, hid_send, hid_recv, part_own, part_send, part_recv, gathered,
-    s_in, s_clip, s_clipf, r_clip, s_text, r_text, s_feat, s_featf, r_feat, s_cg, r_cg, s_tg, r_tg,
+    s_in, s_clip, s_clipf, r_clip, s_text, r_text, s_feat, s_featf, r_feat, s_give, r_give, s_cg, r_cg, s_tg, r_tg,
     s_hid, r_hid, s_part, r_part, s_agz, r_agz, s_agp, r_agp, s_agc, r_agc,
 ):
     depth = blocks // INNER
@@ -126,48 +126,59 @@
         copy(clips.at[a], clips.at[a], s_clipf.at[q], r_clip.at[a], sibling).start()
     peers(half, pos, pass_clip)
 
-    peers(depth, zed, lambda z: got(texts, z, r_text, s_text))
+    def take_clip(q, carry):
+        got(clips, block_at(q, 1 - core), r_clip, s_clip)
+        return carry
+    lax.fori_loop(0, half, take_clip, 0)
 
     scale = scale_ref[0]
     bias = bias_ref[0]
-    all_texts = lambda: texts[...].reshape(depth * rows, width)
-
-    def gate_block(a, own):
-        logits = scale * lax.dot_general(clips[a], all_texts(), NT, preferred_element_type=F32) + bias
-        if own:
-            row = lax.broadcasted_iota(jnp.int32, logits.shape, 0)
-            column = lax.broadcasted_iota(jnp.int32, logits.shape, 1)
-            sign = jnp.where(column - row == zed * rows, 1.0, -1.0)
-            gate = (-sign / (1.0 + jnp.exp(sign * logits))).astype(BF16)
-        else:
-            gate = (1.0 / (1.0 + jnp.exp(-logits))).astype(BF16)
-        gates[a] = gate
-        return jnp.dot(gate, all_texts(), preferred_element_type=F32)
-
-    clip_own[...] = gate_block(me, True)
-
-    def clip_step(a):
-        clip_send[a] = gate_block(a, False).astype(BF16)
-        copy(clip_send.at[a], clip_recv.at[me], s_cg.at[a], r_cg.at[me], at_plane(a)).start()
-    peers(half, pos, lambda q: clip_step(block_at(q, core)))
-
-    def clip_other(q, carry):
-        a = block_at(q, 1 - core)
-        got(clips, a, r_clip, s_clip)
-        clip_step(a)
-        return carry
-    lax.fori_loop(0, half, clip_other, 0)
-
-    def text_term(z):
-        start = pl.multiple_of(z * rows, rows)
-        block = gates[:, :, pl.ds(start, rows)].reshape(plane * rows, rows)
-        return lax.dot_general(
-            block, clips[...].reshape(plane * rows, width), TN, preferred_element_type=F32)
+
+    def all_clips():
+        return clips[...].reshape(plane * rows, width)
+
+    def columns(z):
+        return pl.ds(pl.multiple_of(z * rows, rows), rows)
+
+    def logits_of(z):
+        return scale * lax.dot_general(all_clips(), texts[z], NT, preferred_element_type=F32) + bias
+
+    def text_term(gate):
+        return lax.dot_general(gate, all_clips(), TN, preferred_element_type=F32)
+
+    logits = logits_of(zed)
+    row = lax.broadcasted_iota(jnp.int32, logits.shape, 0)
+    column = lax.broadcasted_iota(jnp.int32, logits.shape, 1)
+    sign = jnp.where(row - column == me * rows, 1.0, -1.0)
+    own_gate = (-sign / (1.0 + jnp.exp(sign * logits))).astype(BF16)
+    gates[:, :, columns(zed)] = own_gate.reshape(plane, rows, rows)
 
     def text_step(z):
-        text_send[z] = text_term(z).astype(BF16)
+        got(texts, z, r_text, s_text)
+        gate = (1.0 / (1.0 + jnp.exp(-logits_of(z)))).astype(BF16)
+        text_send[z] = text_term(gate).astype(BF16)
         copy(text_send.at[z], text_recv.at[zed], s_tg.at[z], r_tg.at[zed], at_depth(z)).start()
+        gates[:, :, columns(z)] = gate.reshape(plane, rows, rows)
     peers(depth, zed, text_step)
+
+    def clip_term(a):
+        return jnp.dot(gates[a], texts[...].reshape(depth * rows, width), preferred_element_type=F32)
+
+    def give_clip(q, carry):
+        clip_give[q] = clip_term(block_at(q, 1 - core)).astype(BF16)
+        copy(clip_give.at[q], clip_take.at[q], s_give.at[q], r_give.at[q], sibling).start()
+        return carry
+    lax.fori_loop(0, half, give_clip, 0)
+
+    def send_sum(q):
+        term = clip_term(block_at(q, core))
+        got(clip_take, q, r_give, s_give)
+        clip_send[q] = (term + clip_take[q].astype(F32)).astype(BF16)
+        copy(clip_send.at[q], clip_recv.at[pos], s_cg.at[q], r_cg.at[pos], at_plane(block_at(q, core))).start()
+    peers(half, pos, send_sum)
+    own_term = clip_term(me)
+    got(clip_take, pos, r_give, s_give)
+    clip_own[...] = own_term + clip_take[pos].astype(F32)
 
     def pass_feat(q):
         a = block_at(q, core)
@@ -175,7 +186,7 @@
         copy(feats.at[a], feats.at[a], s_featf.at[q], r_feat.at[a], sibling).start()
     peers(half, pos, pass_feat)
 
-    text_own[...] = text_term(zed)
+    text_own[...] = text_term(gates[:, :, columns(zed)].reshape(plane * rows, rows))
 
     def backward(at, own, grad):
         unit = units[at]
@@ -188,7 +199,7 @@
     def add_clip(a):
         got(clip_recv, a, r_cg, s_cg)
         clip_own[...] += clip_recv[a].astype(F32)
-    peers(plane, me, add_clip)
+    peers(half, pos, add_clip)
     backward(0, clip_own, clip_own[...])
 
     def send_hid(want, a):
@@ -292,16 +303,17 @@
     def drain_half(q, carry):
         sent(clips.at[me], s_clipf, r_clip, q)
         sent(staged.at[0], s_featf, r_feat, q)
+        sent(clip_give.at[q], s_give, r_give, q)
         return carry
     lax.fori_loop(0, half, drain_half, 0)
 
     def drain_same(q):
         sent(clips.at[me], s_clip, r_clip, q)
         sent(staged.at[0], s_feat, r_feat, q)
+        sent(clip_send.at[q], s_cg, r_cg, q)
     peers(half, pos, drain_same)
 
     def drain_plane(a):
-        sent(clip_send.at[a], s_cg, r_cg, a)
         sent(hid_send.at[0], s_hid, r_hid, a)
     peers(plane, me, drain_plane)
 
@@ -334,7 +346,7 @@
     dma = pltpu.SemaphoreType.DMA
     half = plane // 2
     sems = [dma((count,)) for count in (
-        4, half, half, plane, depth, depth, half, half, plane, plane, plane, depth, depth,
+        4, half, half, plane, depth, depth, half, half, plane, half, half, half, half, depth, depth,
         plane, plane, depth, depth, depth, depth)]
     sems += [dma((4, depth))] * 4
     whole = jax.ShapeDtypeStruct((wide, width), BF16)
@@ -351,8 +363,10 @@
             pltpu.VMEM((2, wide, width), BF16),
             pltpu.VMEM((plane, rows, wide), BF16),
             pltpu.VMEM((plane, rows, depth * rows), BF16),
-            pltpu.VMEM((plane, rows, width), BF16),
-            pltpu.VMEM((plane, rows, width), BF16),
+            pltpu.VMEM((half, rows, width), BF16),
+            pltpu.VMEM((half, rows, width), BF16),
+            pltpu.VMEM((half, rows, width), BF16),
+            pltpu.VMEM((half, rows, width), BF16),
             pltpu.VMEM((depth, rows, width), BF16),
             pltpu.VMEM((depth, rows, width), BF16),
             pltpu.VMEM((rows, width), F32),

time: 71.5 us -> 67.8 us (0.948)
  Pallas kernels: 65.5 us -> 61.8 us
    pallas_call x1, Pallas kernels: 65.5 us -> 61.8 us  [per_device(): pl.pallas_call(functools.partial(kernel, blocks, groups), out_shape=(whol...]
where the time goes in v3:
time: 67.8 us; the launch traced here: 67.6 us
  Pallas kernels  61.8 us (91%)
  other arithmetic  3.92 us (6%)
  between operations  1.94 us (3%)
    pallas_call x1, Pallas kernels, per_device(): pl.pallas_call(functools.partial(kernel, blocks, groups), out_shape=(whol...  61.8 us
    convert_element_type x2, other arithmetic, per_device(): return tuple((grad.astype(F32) for grad in grads))  3.92 us

profile of v3, /device:TPU:11, one launch (start us, length us, event | category | flops | bytes accessed | tf_op | source)
XLA Modules:
  0.0 67.6 jit_solution(13567858517344846479)
XLA Ops:
  1.9 61.8 %shard_map.77 = (bf16[768,512]{1,0:T(8,128)(2,1)}, bf16[768,512]{1,0:T(8,128)(2,1)}) custom-call(bf16[128,768]{1,0:T(8,128)(2,1)} %audio_ref.1, bf16[768,512]{1,0:T(8,128)(2,1)} %audio_w_ref.1, bf16[128,768]{1,0:T(8,128)(2,1)} %text_ref.1, bf16[768,512]{1,0:T(8,128)(2,1)} %text_w_ref.1, f32[1]{0:T(128)S(6)} %copy.8.scale_ref, f32[1]{0:T(128)S(6)} %copy.9.bias_ref), custom_call_target="tpu_custom_call" | custom-call | tf_op jit(solution)/shard_map/pallas_call | solution.py:354
  63.7 0.0 copy-start
  63.7 2.6 %convert_element_type.6 = f32[768,512]{1,0:T(8,128)} convert(bf16[768,512]{1,0:T(8,128)(2,1)} %get-tuple-element.4) | non-fusion elementwise | flops 393216 | bytes 2359296 | tf_op jit(solution)/shard_map/convert_element_type | solution.py:386
  66.3 0.0 copy-done
  66.3 1.4 %convert_element_type.7 = f32[768,512]{1,0:T(8,128)} convert(bf16[768,512]{1,0:T(8,128)(2,1)S(1)} %copy-done) | non-fusion elementwise | flops 393216 | bytes 2359296 | tf_op jit(solution)/shard_map/convert_element_type | solution.py:386
Async XLA Ops:
  63.7 2.6 %copy-start = (bf16[768,512]{1,0:T(8,128)(2,1)S(1)}, bf16[768,512]{1,0:T(8,128)(2,1)}, u32[]{:S(2)}) copy-start(bf16[768,512]{1,0:T(8,128)(2,1)} %get-tuple-element.5) | copy-start | bytes 2359300

commit v4 on v3

--- a/solution.py
+++ b/solution.py
@@ -18,7 +18,7 @@
 def kernel(
     blocks, groups,
     audio_ref, audio_w_ref, text_ref, text_w_ref, scale_ref, bias_ref,
-    audio_out, text_out,
+    out,
     clips, texts, staged, weights, feats, gates, clip_give, clip_take, clip_send, clip_recv, text_send, text_recv,
     clip_own, text_own, units, norms, hid_send, hid_recv, part_own, part_send, part_recv, gathered,
     s_in, s_clip, s_clipf, r_clip, s_text, r_text, s_feat, s_featf, r_feat, s_give, r_give, s_cg, r_cg, s_tg, r_tg,
@@ -94,22 +94,20 @@
     loads[1].wait()
     loads[3].wait()
     texts[zed] = embed(1)
+    loads[0].wait()
+    loads[2].wait()
+    clips[me] = embed(0)
+    feats[me] = staged[kind]
     pl.semaphore_wait(barrier, plane - 1 + depth - 1)
 
     def send_text(z):
         copy(texts.at[zed], texts.at[zed], s_text.at[z], r_text.at[zed], at_depth(z)).start()
     peers(depth, zed, send_text)
-
-    loads[0].wait()
-    loads[2].wait()
-    clips[me] = embed(0)
 
     def send_clip(q):
         copy(clips.at[me], clips.at[me], s_clip.at[q], r_clip.at[me], at_plane(block_at(q, core))).start()
     peers(half, pos, send_clip)
     copy(clips.at[me], clips.at[me], s_clipf.at[pos], r_clip.at[me], sibling).start()
-
-    feats[me] = staged[kind]
 
     def send_feat(q):
         a = block_at(q, core)
@@ -235,70 +233,9 @@
         copy(part_send.at[z], part_recv.at[zed], s_part.at[z], r_part.at[zed], at_depth(z)).start()
     peers(depth, zed, send_part)
     part_recv[zed] = jnp.zeros(part_recv.shape[1:], BF16)
-    peers(depth, zed, lambda z: got(part_recv, z, r_part, s_part))
-    total = part_own[zed]
-    for z in range(depth):
-        total = total + part_recv[z].astype(F32)
-
-    def piece(q, c, z):
-        return gathered.at[lax.div(q, 2), lax.rem(q, 2) * 2 + c, pl.ds(pl.multiple_of(z * span, span), span)]
-
-    own = kind * 2 + lax.div(inner, 2)
-    near = lax.div(group, 2) * 2
-    gathered[kind, inner, pl.ds(pl.multiple_of(zed * span, span), span)] = total.astype(BF16)
-
-    def same_core(q):
-        return (zed * INNER + lax.rem(q, 2) * 2 + core, near + lax.div(q, 2))
-
-    def send_z(z):
-        here = piece(own, core, zed)
-        copy(here, here, s_agz.at[z], r_agz.at[zed], at_depth(z)).start()
-    peers(depth, zed, send_z)
-
-    def to_sibling(q, z):
-        here = piece(q, core, z)
-        copy(here, here, s_agc.at[q, z], r_agc.at[q, z], sibling).start()
-
-    def spread(z):
-        here = piece(own, core, z)
-
-        def send(q):
-            copy(here, here, s_agp.at[q, z], r_agp.at[own, z], same_core(q)).start()
-        peers(4, own, send)
-        to_sibling(own, z)
-
-    spread(zed)
-
-    def take_z(z):
-        here = piece(own, core, z)
-        copy(here, here, s_agz.at[z], r_agz.at[z], (blk, group)).wait_recv()
-        spread(z)
-    peers(depth, zed, take_z)
-
-    def relay(k, carry):
-        z = lax.rem(zed + k, depth)
-
-        def take(q):
-            here = piece(q, core, z)
-            copy(here, here, s_agp.at[q, z], r_agp.at[q, z], (blk, group)).wait_recv()
-            to_sibling(q, z)
-        peers(4, own, take)
-        return carry
-    lax.fori_loop(0, depth, relay, 0)
-
-    def finish(k, carry):
-        z = lax.rem(zed + k, depth)
-        for q in range(4):
-            there = piece(q, 1 - core, z)
-            copy(there, there, s_agc.at[q, z], r_agc.at[q, z], sibling).wait_recv()
-        return carry
-    lax.fori_loop(0, depth, finish, 0)
-    for p in range(4):
-        audio_out[:, p * lanes:(p + 1) * lanes] = gathered[0, p]
-        text_out[:, p * lanes:(p + 1) * lanes] = gathered[1, p]
 
     def sent(src, send, recv, at):
-        copy(src, src, send.at[at], recv.at[at], (blk, group)).wait_send()
+        copy(src, src, send.at[at], recv.at[0], (blk, group)).wait_send()
 
     def drain_half(q, carry):
         sent(clips.at[me], s_clipf, r_clip, q)
@@ -312,28 +249,77 @@
         sent(staged.at[0], s_feat, r_feat, q)
         sent(clip_send.at[q], s_cg, r_cg, q)
     peers(half, pos, drain_same)
-
-    def drain_plane(a):
-        sent(hid_send.at[0], s_hid, r_hid, a)
-    peers(plane, me, drain_plane)
+    peers(plane, me, lambda a: sent(hid_send.at[0], s_hid, r_hid, a))
 
     def drain_depth(z):
         sent(texts.at[zed], s_text, r_text, z)
         sent(text_send.at[z], s_tg, r_tg, z)
+    peers(depth, zed, drain_depth)
+
+    peers(depth, zed, lambda z: got(part_recv, z, r_part, s_part))
+    total = part_own[zed]
+    for z in range(depth):
+        total = total + part_recv[z].astype(F32)
+
+    def rows_of(z):
+        return pl.ds(pl.multiple_of(z * span, span), span)
+
+    own = kind * 2 + lax.div(inner, 2)
+    near = lax.div(group, 2) * 2
+    gathered[core, own, rows_of(zed)] = total.astype(BF16)
+
+    def same_core(q):
+        return (zed * INNER + lax.rem(q, 2) * 2 + core, near + lax.div(q, 2))
+
+    def spread(z):
+        here = gathered.at[core, own, rows_of(z)]
+        peers(4, own, lambda q: copy(here, here, s_agp.at[0], r_agp.at[z], same_core(q)).start())
+
+    def send_z(z):
+        here = gathered.at[core, own, rows_of(zed)]
+        copy(here, here, s_agz.at[z], r_agz.at[zed], at_depth(z)).start()
+    peers(depth, zed, send_z)
+    spread(zed)
+
+    def take_z(z):
+        here = gathered.at[core, own, rows_of(z)]
+        copy(here, here, s_agz.at[z], r_agz.at[z], (blk, group)).wait_recv()
+        spread(z)
+    peers(depth, zed, take_z)
+
+    def relay(k, carry):
+        z = lax.rem(zed + k, depth)
+        three = gathered.at[core, pl.ds(0, 3), rows_of(z)]
+        copy(three, three, s_agp.at[0], r_agp.at[z], (blk, group)).wait_recv()
+        here = gathered.at[core, :, rows_of(z)]
+        copy(here, here, s_agc.at[z], r_agc.at[z], sibling).start()
+        return carry
+    lax.fori_loop(0, depth, relay, 0)
+
+    def place(c):
+        for q in range(4):
+            at = pl.multiple_of(((q % 2) * 2 + c) * lanes, lanes)
+            out[q // 2, :, pl.ds(at, lanes)] = gathered[c, q]
+    place(core)
+
+    def finish(k, carry):
+        z = lax.rem(zed + k, depth)
+        there = gathered.at[1 - core, :, rows_of(z)]
+        copy(there, there, s_agc.at[z], r_agc.at[z], sibling).wait_recv()
+        return carry
+    lax.fori_loop(0, depth, finish, 0)
+    place(1 - core)
+
+    def drain_out(z):
         sent(part_send.at[z], s_part, r_part, z)
-        sent(piece(own, core, zed), s_agz, r_agz, z)
-    peers(depth, zed, drain_depth)
-
-    def drain_out(z, carry):
-        def one(q):
-            here = piece(own, core, z)
-            copy(here, here, s_agp.at[q, z], r_agp.at[q, z], (blk, group)).wait_send()
-        peers(4, own, one)
-        for q in range(4):
-            here = piece(q, core, z)
-            copy(here, here, s_agc.at[q, z], r_agc.at[q, z], sibling).wait_send()
-        return carry
-    lax.fori_loop(0, depth, drain_out, 0)
+        sent(gathered.at[core, own, rows_of(zed)], s_agz, r_agz, z)
+    peers(depth, zed, drain_out)
+    sent(gathered.at[core, pl.ds(0, 3)], s_agp, r_agp, 0)
+
+    def drain_relay(z, carry):
+        sent(gathered.at[core, :, rows_of(z)], s_agc, r_agc, z)
+        return carry
+    lax.fori_loop(0, depth, drain_relay, 0)
 
 
 def per_device(blocks, groups, audio, audio_w, text, text_w, scale, bias):
@@ -348,14 +334,14 @@
     sems = [dma((count,)) for count in (
         4, half, half, plane, depth, depth, half, half, plane, half, half, half, half, depth, depth,
         plane, plane, depth, depth, depth, depth)]
-    sems += [dma((4, depth))] * 4
-    whole = jax.ShapeDtypeStruct((wide, width), BF16)
+    sems += [dma((count,)) for count in (1, depth, depth, depth)]
+    whole = jax.ShapeDtypeStruct((2, wide, width), BF16)
     hbm = pl.BlockSpec(memory_space=pl.ANY)
     grads = pl.pallas_call(
         functools.partial(kernel, blocks, groups),
-        out_shape=(whole, whole),
+        out_shape=whole,
         in_specs=[hbm, hbm, hbm, hbm, smem, smem],
-        out_specs=(vmem, vmem),
+        out_specs=vmem,
         scratch_shapes=[
             pltpu.VMEM((plane, rows, width), BF16),
             pltpu.VMEM((depth, rows, width), BF16),
@@ -383,7 +369,7 @@
         compiler_params=pltpu.CompilerParams(
             collective_id=0, has_side_effects=True, vmem_limit_bytes=56 * 1024 * 1024),
     )(audio, audio_w, text, text_w, scale, bias)
-    return tuple(grad.astype(F32) for grad in grads)
+    return grads[0].astype(F32), grads[1].astype(F32)
 
 
 def solution(mesh):

time: 67.8 us -> 66.7 us (0.984)
  Pallas kernels: 61.8 us -> 61.1 us
    convert_element_type x2 -> x1, other arithmetic: 3.92 us -> 3.48 us  [per_device(): return (grads[0].astype(F32), grads[1].astype(F32))]
where the time goes in v4:
time: 66.7 us; the launch traced here: 66.5 us
  Pallas kernels  61.1 us (92%)
  other arithmetic  3.48 us (5%)
  between operations  1.93 us (3%)
    pallas_call x1, Pallas kernels, per_device(): pl.pallas_call(functools.partial(kernel, blocks, groups), out_shape=whole...  61.1 us
    convert_element_type x1, other arithmetic, per_device(): return (grads[0].astype(F32), grads[1].astype(F32))  3.48 us

profile of v4, /device:TPU:11, one launch (start us, length us, event | category | flops | bytes accessed | tf_op | source)
XLA Modules:
  0.0 66.5 jit_solution(6276629046241470531)
XLA Ops:
  1.9 61.1 %shard_map.77 = bf16[2,768,512]{2,1,0:T(8,128)(2,1)} custom-call(bf16[128,768]{1,0:T(8,128)(2,1)} %audio_ref.1, bf16[768,512]{1,0:T(8,128)(2,1)} %audio_w_ref.1, bf16[128,768]{1,0:T(8,128)(2,1)} %text_ref.1, bf16[768,512]{1,0:T(8,128)(2,1)} %text_w_ref.1, f32[1]{0:T(128)S(6)} %copy.8.scale_ref, f32[1]{0:T(128)S(6)} %copy.9.bias_ref), custom_call_target="tpu_custom_call" | custom-call | tf_op jit(solution)/shard_map/pallas_call | solution.py:340
  63.1 3.5 %bitcast_convert_fusion = (f32[768,512]{1,0:T(8,128)}, f32[768,512]{1,0:T(8,128)}) fusion(bf16[2,768,512]{2,1,0:T(8,128)(2,1)} %shard_map.77), kind=kLoop, calls=%fused_computation | loop fusion | flops 786432 | bytes 4718592 | tf_op jit(solution)/shard_map/convert_element_type | solution.py:372

commit v5 on v4

--- a/solution.py
+++ b/solution.py
@@ -21,8 +21,8 @@
     out,
     clips, texts, staged, weights, feats, gates, clip_give, clip_take, clip_send, clip_recv, text_send, text_recv,
     clip_own, text_own, units, norms, hid_send, hid_recv, part_own, part_send, part_recv, gathered,
-    s_in, s_clip, s_clipf, r_clip, s_text, r_text, s_feat, s_featf, r_feat, s_give, r_give, s_cg, r_cg, s_tg, r_tg,
-    s_hid, r_hid, s_part, r_part, s_agz, r_agz, s_agp, r_agp, s_agc, r_agc,
+    s_in, s_clip, s_clipf, r_clip, s_text, s_textd, r_text, s_feat, s_featf, r_feat, s_give, r_give, s_cg, r_cg, s_tg, r_tg,
+    s_hid, r_hid, s_part, r_part, s_agz, s_agzd, r_agz, s_agp, r_agp, s_agc, r_agc,
 ):
     depth = blocks // INNER
     plane = INNER * groups
@@ -74,6 +74,47 @@
             return carry
         lax.fori_loop(1, count, body, 0)
 
+    def nearest(fn, low, high):
+        def body(d, carry):
+            pl.when(zed >= d)(lambda: fn(zed - d))
+            pl.when(zed + d < depth)(lambda: fn(zed + d))
+            return carry
+        lax.fori_loop(low, high, body, 0)
+
+    class Chain:
+        def __init__(self, block, up, down, recv):
+            self.block, self.up, self.down, self.recv = block, up, down, recv
+
+        def forward(self, b):
+            here = self.block(b)
+
+            @pl.when(jnp.logical_and(b <= zed, zed + 1 < depth))
+            def _():
+                copy(here, here, self.up.at[b], self.recv.at[b], at_depth(zed + 1)).start()
+
+            @pl.when(jnp.logical_and(b >= zed, zed > 0))
+            def _():
+                copy(here, here, self.down.at[b], self.recv.at[b], at_depth(zed - 1)).start()
+
+        def take(self, b):
+            here = self.block(b)
+            copy(here, here, self.up.at[b], self.recv.at[b], (blk, group)).wait_recv()
+            self.forward(b)
+
+        def drain(self):
+            def body(b, carry):
+                here = self.block(b)
+
+                @pl.when(jnp.logical_and(b <= zed, zed + 1 < depth))
+                def _():
+                    copy(here, here, self.up.at[b], self.recv.at[b], (blk, group)).wait_send()
+
+                @pl.when(jnp.logical_and(b >= zed, zed > 0))
+                def _():
+                    copy(here, here, self.down.at[b], self.recv.at[b], (blk, group)).wait_send()
+                return carry
+            lax.fori_loop(0, depth, body, 0)
+
     mine = role(me)
     kind = kind_of(me)
 
@@ -100,14 +141,23 @@
     feats[me] = staged[kind]
     pl.semaphore_wait(barrier, plane - 1 + depth - 1)
 
-    def send_text(z):
-        copy(texts.at[zed], texts.at[zed], s_text.at[z], r_text.at[zed], at_depth(z)).start()
-    peers(depth, zed, send_text)
+    text_chain = Chain(lambda z: texts.at[z], s_text, s_textd, r_text)
+    text_chain.forward(zed)
 
     def send_clip(q):
         copy(clips.at[me], clips.at[me], s_clip.at[q], r_clip.at[me], at_plane(block_at(q, core))).start()
     peers(half, pos, send_clip)
     copy(clips.at[me], clips.at[me], s_clipf.at[pos], r_clip.at[me], sibling).start()
+
+    def got(buf, at, recv, send):
+        copy(buf.at[at], buf.at[at], send.at[0], recv.at[at], (blk, group)).wait_recv()
+
+    def pass_clip(q):
+        a = block_at(q, core)
+        got(clips, a, r_clip, s_clip)
+        copy(clips.at[a], clips.at[a], s_clipf.at[q], r_clip.at[a], sibling).start()
+    nearest(text_chain.take, 1, min(2, depth))
+    peers(half, pos, pass_clip)
 
     def send_feat(q):
         a = block_at(q, core)
@@ -115,14 +165,7 @@
     peers(half, pos, send_feat)
     copy(staged.at[kind], feats.at[me], s_featf.at[pos], r_feat.at[me], sibling).start()
 
-    def got(buf, at, recv, send):
-        copy(buf.at[at], buf.at[at], send.at[0], recv.at[at], (blk, group)).wait_recv()
-
-    def pass_clip(q):
-        a = block_at(q, core)
-        got(clips, a, r_clip, s_clip)
-        copy(clips.at[a], clips.at[a], s_clipf.at[q], r_clip.at[a], sibling).start()
-    peers(half, pos, pass_clip)
+    nearest(text_chain.take, 2, min(3, depth))
 
     def take_clip(q, carry):
         got(clips, block_at(q, 1 - core), r_clip, s_clip)
@@ -152,12 +195,16 @@
     gates[:, :, columns(zed)] = own_gate.reshape(plane, rows, rows)
 
     def text_step(z):
-        got(texts, z, r_text, s_text)
         gate = (1.0 / (1.0 + jnp.exp(-logits_of(z)))).astype(BF16)
         text_send[z] = text_term(gate).astype(BF16)
         copy(text_send.at[z], text_recv.at[zed], s_tg.at[z], r_tg.at[zed], at_depth(z)).start()
         gates[:, :, columns(z)] = gate.reshape(plane, rows, rows)
-    peers(depth, zed, text_step)
+
+    def late_step(z):
+        text_chain.take(z)
+        text_step(z)
+    nearest(text_step, 1, min(3, depth))
+    nearest(late_step, 3, depth)
 
     def clip_term(a):
         return jnp.dot(gates[a], texts[...].reshape(depth * rows, width), preferred_element_type=F32)
@@ -252,10 +299,10 @@
     peers(plane, me, lambda a: sent(hid_send.at[0], s_hid, r_hid, a))
 
     def drain_depth(z):
-        sent(texts.at[zed], s_text, r_text, z)
         sent(text_send.at[z], s_tg, r_tg, z)
     peers(depth, zed, drain_depth)
 
+    text_chain.drain()
     peers(depth, zed, lambda z: got(part_recv, z, r_part, s_part))
     total = part_own[zed]
     for z in range(depth):
@@ -275,26 +322,22 @@
         here = gathered.at[core, own, rows_of(z)]
         peers(4, own, lambda q: copy(here, here, s_agp.at[0], r_agp.at[z], same_core(q)).start())
 
-    def send_z(z):
-        here = gathered.at[core, own, rows_of(zed)]
-        copy(here, here, s_agz.at[z], r_agz.at[zed], at_depth(z)).start()
-    peers(depth, zed, send_z)
+    out_chain = Chain(lambda z: gathered.at[core, own, rows_of(z)], s_agz, s_agzd, r_agz)
+    out_chain.forward(zed)
     spread(zed)
 
     def take_z(z):
-        here = gathered.at[core, own, rows_of(z)]
-        copy(here, here, s_agz.at[z], r_agz.at[z], (blk, group)).wait_recv()
+        out_chain.take(z)
         spread(z)
-    peers(depth, zed, take_z)
-
-    def relay(k, carry):
-        z = lax.rem(zed + k, depth)
+    nearest(take_z, 1, depth)
+
+    def relay(z):
         three = gathered.at[core, pl.ds(0, 3), rows_of(z)]
         copy(three, three, s_agp.at[0], r_agp.at[z], (blk, group)).wait_recv()
         here = gathered.at[core, :, rows_of(z)]
         copy(here, here, s_agc.at[z], r_agc.at[z], sibling).start()
-        return carry
-    lax.fori_loop(0, depth, relay, 0)
+    relay(zed)
+    nearest(relay, 1, depth)
 
     def place(c):
         for q in range(4):
@@ -312,14 +355,19 @@
 
     def drain_out(z):
         sent(part_send.at[z], s_part, r_part, z)
-        sent(gathered.at[core, own, rows_of(zed)], s_agz, r_agz, z)
     peers(depth, zed, drain_out)
+    out_chain.drain()
     sent(gathered.at[core, pl.ds(0, 3)], s_agp, r_agp, 0)
 
     def drain_relay(z, carry):
         sent(gathered.at[core, :, rows_of(z)], s_agc, r_agc, z)
         return carry
     lax.fori_loop(0, depth, drain_relay, 0)
+
+
+def widen(grads_ref, audio_ref, text_ref):
+    audio_ref[...] = grads_ref[0].astype(F32)
+    text_ref[...] = grads_ref[1].astype(F32)
 
 
 def per_device(blocks, groups, audio, audio_w, text, text_w, scale, bias):
@@ -332,8 +380,8 @@
     dma = pltpu.SemaphoreType.DMA
     half = plane // 2
     sems = [dma((count,)) for count in (
-        4, half, half, plane, depth, depth, half, half, plane, half, half, half, half, depth, depth,
-        plane, plane, depth, depth, depth, depth)]
+        4, half, half, plane, depth, depth, depth, half, half, plane, half, half, half, half, depth, depth,
+        plane, plane, depth, depth, depth, depth, depth)]
     sems += [dma((count,)) for count in (1, depth, depth, depth)]
     whole = jax.ShapeDtypeStruct((2, wide, width), BF16)
     hbm = pl.BlockSpec(memory_space=pl.ANY)
@@ -369,7 +417,15 @@
         compiler_params=pltpu.CompilerParams(
             collective_id=0, has_side_effects=True, vmem_limit_bytes=56 * 1024 * 1024),
     )(audio, audio_w, text, text_w, scale, bias)
-    return grads[0].astype(F32), grads[1].astype(F32)
+    full = jax.ShapeDtypeStruct((wide, width), F32)
+    step = wide // 4
+    return pl.pallas_call(
+        widen,
+        out_shape=(full, full),
+        grid=(4,),
+        in_specs=[pl.BlockSpec((2, step, width), lambda i: (0, i, 0))],
+        out_specs=(pl.BlockSpec((step, width), lambda i: (i, 0)),) * 2,
+    )(grads)
 
 
 def solution(mesh):

time: 66.7 us -> 68.1 us (1.021)
  the two profiles are of different devices: /device:TPU:11 before, /device:TPU:1 now
where the time goes in v5:
time: 68.1 us; the launch traced here: 67.8 us
  Pallas kernels  65.9 us (97%)
  between operations  1.93 us (3%)
    pallas_call x1, Pallas kernels, per_device(): pl.pallas_call(functools.partial(kernel, blocks, groups), out_shape=whole...  62.1 us
    pallas_call x1, Pallas kernels, per_device(): pl.pallas_call(widen, out_shape=(full, full), grid=(4,), in_specs=[pl.Blo...  3.85 us

profile of v5, /device:TPU:1, one launch (start us, length us, event | category | flops | bytes accessed | tf_op | source)
XLA Modules:
  0.0 67.8 jit_solution(16034410020151930687)
XLA Ops:
  1.9 62.1 %shard_map.77.grads_ref = bf16[2,768,512]{2,1,0:T(8,128)(2,1)} custom-call(bf16[128,768]{1,0:T(8,128)(2,1)} %audio_ref.1, bf16[768,512]{1,0:T(8,128)(2,1)} %audio_w_ref.1, bf16[128,768]{1,0:T(8,128)(2,1)} %text_ref.1, bf16[768,512]{1,0:T(8,128)(2,1)} %text_w_ref.1, f32[1]{0:T(128)S(6)} %copy.8.scale_ref, f32[1]{0:T(128)S(6)} %copy.9.bias_ref), custom_call_target="tpu_custom_call" | custom-call | tf_op jit(solution)/shard_map/pallas_call | solution.py:388
  64.0 3.9 %shard_map.78 = (f32[768,512]{1,0:T(8,128)}, f32[768,512]{1,0:T(8,128)}) custom-call(bf16[2,768,512]{2,1,0:T(8,128)(2,1)} %shard_map.77.grads_ref), custom_call_target="tpu_custom_call" | custom-call | tf_op jit(solution)/shard_map/pallas_call | solution.py:422

commit v6 on v4

--- a/solution.py
+++ b/solution.py
@@ -109,20 +109,20 @@
     peers(half, pos, send_clip)
     copy(clips.at[me], clips.at[me], s_clipf.at[pos], r_clip.at[me], sibling).start()
 
+    def got(buf, at, recv, send):
+        copy(buf.at[at], buf.at[at], send.at[0], recv.at[at], (blk, group)).wait_recv()
+
+    def pass_clip(q):
+        a = block_at(q, core)
+        got(clips, a, r_clip, s_clip)
+        copy(clips.at[a], clips.at[a], s_clipf.at[q], r_clip.at[a], sibling).start()
+    peers(half, pos, pass_clip)
+
     def send_feat(q):
         a = block_at(q, core)
         copy(staged.at[kind_of(a)], feats.at[me], s_feat.at[q], r_feat.at[me], at_plane(a)).start()
     peers(half, pos, send_feat)
     copy(staged.at[kind], feats.at[me], s_featf.at[pos], r_feat.at[me], sibling).start()
-
-    def got(buf, at, recv, send):
-        copy(buf.at[at], buf.at[at], send.at[0], recv.at[at], (blk, group)).wait_recv()
-
-    def pass_clip(q):
-        a = block_at(q, core)
-        got(clips, a, r_clip, s_clip)
-        copy(clips.at[a], clips.at[a], s_clipf.at[q], r_clip.at[a], sibling).start()
-    peers(half, pos, pass_clip)
 
     def take_clip(q, carry):
         got(clips, block_at(q, 1 - core), r_clip, s_clip)
@@ -229,9 +229,17 @@
     part_own[...] = terms
     part_send[...] = terms.astype(BF16)
 
-    def send_part(z):
-        copy(part_send.at[z], part_recv.at[zed], s_part.at[z], r_part.at[zed], at_depth(z)).start()
-    peers(depth, zed, send_part)
+    short = span // 2
+
+    def half_rows(h):
+        return pl.ds(h * short, short)
+
+    def send_part(h, z):
+        at = 2 * z + h
+        copy(part_send.at[z, half_rows(h)], part_recv.at[zed, half_rows(h)],
+             s_part.at[at], r_part.at[2 * zed + h], at_depth(z)).start()
+    for h in range(2):
+        peers(depth, zed, functools.partial(send_part, h))
     part_recv[zed] = jnp.zeros(part_recv.shape[1:], BF16)
 
     def sent(src, send, recv, at):
@@ -256,45 +264,54 @@
         sent(text_send.at[z], s_tg, r_tg, z)
     peers(depth, zed, drain_depth)
 
-    peers(depth, zed, lambda z: got(part_recv, z, r_part, s_part))
-    total = part_own[zed]
-    for z in range(depth):
-        total = total + part_recv[z].astype(F32)
-
-    def rows_of(z):
-        return pl.ds(pl.multiple_of(z * span, span), span)
+    def rows_of(z, h):
+        return pl.ds(pl.multiple_of(z * span + h * short, short), short)
 
     own = kind * 2 + lax.div(inner, 2)
     near = lax.div(group, 2) * 2
-    gathered[core, own, rows_of(zed)] = total.astype(BF16)
 
     def same_core(q):
         return (zed * INNER + lax.rem(q, 2) * 2 + core, near + lax.div(q, 2))
 
-    def spread(z):
-        here = gathered.at[core, own, rows_of(z)]
-        peers(4, own, lambda q: copy(here, here, s_agp.at[0], r_agp.at[z], same_core(q)).start())
-
-    def send_z(z):
-        here = gathered.at[core, own, rows_of(zed)]
-        copy(here, here, s_agz.at[z], r_agz.at[zed], at_depth(z)).start()
-    peers(depth, zed, send_z)
-    spread(zed)
-
-    def take_z(z):
-        here = gathered.at[core, own, rows_of(z)]
-        copy(here, here, s_agz.at[z], r_agz.at[z], (blk, group)).wait_recv()
-        spread(z)
-    peers(depth, zed, take_z)
-
-    def relay(k, carry):
+    def spread(h, z):
+        here = gathered.at[core, own, rows_of(z, h)]
+        at = 2 * z + h
+        peers(4, own, lambda q: copy(here, here, s_agp.at[0], r_agp.at[at], same_core(q)).start())
+
+    def take_part(h, z):
+        here = part_recv.at[z, half_rows(h)]
+        copy(here, here, s_part.at[0], r_part.at[2 * z + h], (blk, group)).wait_recv()
+
+    def send_z(h, z):
+        here = gathered.at[core, own, rows_of(zed, h)]
+        copy(here, here, s_agz.at[2 * z + h], r_agz.at[2 * zed + h], at_depth(z)).start()
+
+    def take_z(h, z):
+        here = gathered.at[core, own, rows_of(z, h)]
+        copy(here, here, s_agz.at[2 * z + h], r_agz.at[2 * z + h], (blk, group)).wait_recv()
+        spread(h, z)
+
+    def relay(h, k, carry):
         z = lax.rem(zed + k, depth)
-        three = gathered.at[core, pl.ds(0, 3), rows_of(z)]
-        copy(three, three, s_agp.at[0], r_agp.at[z], (blk, group)).wait_recv()
-        here = gathered.at[core, :, rows_of(z)]
-        copy(here, here, s_agc.at[z], r_agc.at[z], sibling).start()
-        return carry
-    lax.fori_loop(0, depth, relay, 0)
+        at = 2 * z + h
+        three = gathered.at[core, pl.ds(0, 3), rows_of(z, h)]
+        copy(three, three, s_agp.at[0], r_agp.at[at], (blk, group)).wait_recv()
+        here = gathered.at[core, :, rows_of(z, h)]
+        copy(here, here, s_agc.at[at], r_agc.at[at], sibling).start()
+        return carry
+
+    for h in range(2):
+        peers(depth, zed, functools.partial(take_part, h))
+        total = part_own[zed, h * short:(h + 1) * short]
+        for z in range(depth):
+            total = total + part_recv[z, h * short:(h + 1) * short].astype(F32)
+        gathered[core, own, rows_of(zed, h)] = total.astype(BF16)
+        peers(depth, zed, functools.partial(send_z, h))
+        spread(h, zed)
+    for h in range(2):
+        peers(depth, zed, functools.partial(take_z, h))
+    for h in range(2):
+        lax.fori_loop(0, depth, functools.partial(relay, h), 0)
 
     def place(c):
         for q in range(4):
@@ -302,24 +319,26 @@
             out[q // 2, :, pl.ds(at, lanes)] = gathered[c, q]
     place(core)
 
-    def finish(k, carry):
+    def finish(h, k, carry):
         z = lax.rem(zed + k, depth)
-        there = gathered.at[1 - core, :, rows_of(z)]
-        copy(there, there, s_agc.at[z], r_agc.at[z], sibling).wait_recv()
-        return carry
-    lax.fori_loop(0, depth, finish, 0)
+        there = gathered.at[1 - core, :, rows_of(z, h)]
+        copy(there, there, s_agc.at[2 * z + h], r_agc.at[2 * z + h], sibling).wait_recv()
+        return carry
+    for h in range(2):
+        lax.fori_loop(0, depth, functools.partial(finish, h), 0)
     place(1 - core)
 
-    def drain_out(z):
-        sent(part_send.at[z], s_part, r_part, z)
-        sent(gathered.at[core, own, rows_of(zed)], s_agz, r_agz, z)
-    peers(depth, zed, drain_out)
+    def drain_out(h, z):
+        sent(part_send.at[z, half_rows(h)], s_part, r_part, 2 * z + h)
+        sent(gathered.at[core, own, rows_of(zed, h)], s_agz, r_agz, 2 * z + h)
+
+    def drain_relay(h, z, carry):
+        sent(gathered.at[core, :, rows_of(z, h)], s_agc, r_agc, 2 * z + h)
+        return carry
+    for h in range(2):
+        peers(depth, zed, functools.partial(drain_out, h))
+        lax.fori_loop(0, depth, functools.partial(drain_relay, h), 0)
     sent(gathered.at[core, pl.ds(0, 3)], s_agp, r_agp, 0)
-
-    def drain_relay(z, carry):
-        sent(gathered.at[core, :, rows_of(z)], s_agc, r_agc, z)
-        return carry
-    lax.fori_loop(0, depth, drain_relay, 0)
 
 
 def per_device(blocks, groups, audio, audio_w, text, text_w, scale, bias):
@@ -333,8 +352,8 @@
     half = plane // 2
     sems = [dma((count,)) for count in (
         4, half, half, plane, depth, depth, half, half, plane, half, half, half, half, depth, depth,
-        plane, plane, depth, depth, depth, depth)]
-    sems += [dma((count,)) for count in (1, depth, depth, depth)]
+        plane, plane, 2 * depth, 2 * depth, 2 * depth, 2 * depth)]
+    sems += [dma((count,)) for count in (1, 2 * depth, 2 * depth, 2 * depth)]
     whole = jax.ShapeDtypeStruct((2, wide, width), BF16)
     hbm = pl.BlockSpec(memory_space=pl.ANY)
     grads = pl.pallas_call(

time: 66.7 us -> 63.1 us (0.946)
  Pallas kernels: 61.1 us -> 57.5 us
    pallas_call x1, Pallas kernels: 61.1 us -> 57.5 us  [per_device(): pl.pallas_call(functools.partial(kernel, blocks, groups), out_shape=whole...]
where the time goes in v6:
time: 63.1 us; the launch traced here: 62.9 us
  Pallas kernels  57.5 us (91%)
  other arithmetic  3.48 us (6%)
  between operations  1.93 us (3%)
    pallas_call x1, Pallas kernels, per_device(): pl.pallas_call(functools.partial(kernel, blocks, groups), out_shape=whole...  57.5 us
    convert_element_type x1, other arithmetic, per_device(): return (grads[0].astype(F32), grads[1].astype(F32))  3.48 us

profile of v6, /device:TPU:11, one launch (start us, length us, event | category | flops | bytes accessed | tf_op | source)
XLA Modules:
  0.0 62.9 jit_solution(10316500707505476797)
XLA Ops:
  1.9 57.5 %shard_map.77 = bf16[2,768,512]{2,1,0:T(8,128)(2,1)} custom-call(bf16[128,768]{1,0:T(8,128)(2,1)} %audio_ref.1, bf16[768,512]{1,0:T(8,128)(2,1)} %audio_w_ref.1, bf16[128,768]{1,0:T(8,128)(2,1)} %text_ref.1, bf16[768,512]{1,0:T(8,128)(2,1)} %text_w_ref.1, f32[1]{0:T(128)S(6)} %copy.8.scale_ref, f32[1]{0:T(128)S(6)} %copy.9.bias_ref), custom_call_target="tpu_custom_call" | custom-call | tf_op jit(solution)/shard_map/pallas_call | solution.py:359
  59.5 3.5 %bitcast_convert_fusion = (f32[768,512]{1,0:T(8,128)}, f32[768,512]{1,0:T(8,128)}) fusion(bf16[2,768,512]{2,1,0:T(8,128)(2,1)} %shard_map.77), kind=kLoop, calls=%fused_computation | loop fusion | flops 786432 | bytes 4718592 | tf_op jit(solution)/shard_map/convert_element_type | solution.py:391

commit v7 on v6

--- a/solution.py
+++ b/solution.py
@@ -162,11 +162,11 @@
     def clip_term(a):
         return jnp.dot(gates[a], texts[...].reshape(depth * rows, width), preferred_element_type=F32)
 
-    def give_clip(q, carry):
+    def give_clip(q):
         clip_give[q] = clip_term(block_at(q, 1 - core)).astype(BF16)
         copy(clip_give.at[q], clip_take.at[q], s_give.at[q], r_give.at[q], sibling).start()
-        return carry
-    lax.fori_loop(0, half, give_clip, 0)
+    peers(half, pos, give_clip)
+    give_clip(pos)
 
     def send_sum(q):
         term = clip_term(block_at(q, core))
@@ -178,12 +178,6 @@
     got(clip_take, pos, r_give, s_give)
     clip_own[...] = own_term + clip_take[pos].astype(F32)
 
-    def pass_feat(q):
-        a = block_at(q, core)
-        got(feats, a, r_feat, s_feat)
-        copy(feats.at[a], feats.at[a], s_featf.at[q], r_feat.at[a], sibling).start()
-    peers(half, pos, pass_feat)
-
     text_own[...] = text_term(gates[:, :, columns(zed)].reshape(plane * rows, rows))
 
     def backward(at, own, grad):
@@ -205,6 +199,12 @@
         def _():
             copy(hid_send.at[role(a)], hid_recv.at[me], s_hid.at[a], r_hid.at[me], at_plane(a)).start()
     peers(plane, me, functools.partial(send_hid, 0))
+
+    def pass_feat(q):
+        a = block_at(q, core)
+        got(feats, a, r_feat, s_feat)
+        copy(feats.at[a], feats.at[a], s_featf.at[q], r_feat.at[a], sibling).start()
+    peers(half, pos, pass_feat)
 
     def add_text(z):
         got(text_recv, z, r_tg, s_tg)

time: 63.1 us -> 63.1 us (level)
  no operation moved by 1% of the time
where the time goes in v7:
time: 63.1 us; the launch traced here: 62.8 us
  Pallas kernels  57.4 us (91%)
  other arithmetic  3.48 us (6%)
  between operations  1.93 us (3%)
    pallas_call x1, Pallas kernels, per_device(): pl.pallas_call(functools.partial(kernel, blocks, groups), out_shape=whole...  57.4 us
    convert_element_type x1, other arithmetic, per_device(): return (grads[0].astype(F32), grads[1].astype(F32))  3.48 us

profile of v7, /device:TPU:11, one launch (start us, length us, event | category | flops | bytes accessed | tf_op | source)
XLA Modules:
  0.0 62.8 jit_solution(2158577337583401640)
XLA Ops:
  1.9 57.4 %shard_map.77 = bf16[2,768,512]{2,1,0:T(8,128)(2,1)} custom-call(bf16[128,768]{1,0:T(8,128)(2,1)} %audio_ref.1, bf16[768,512]{1,0:T(8,128)(2,1)} %audio_w_ref.1, bf16[128,768]{1,0:T(8,128)(2,1)} %text_ref.1, bf16[768,512]{1,0:T(8,128)(2,1)} %text_w_ref.1, f32[1]{0:T(128)S(6)} %copy.8.scale_ref, f32[1]{0:T(128)S(6)} %copy.9.bias_ref), custom_call_target="tpu_custom_call" | custom-call | tf_op jit(solution)/shard_map/pallas_call | solution.py:359
  59.3 3.5 %bitcast_convert_fusion = (f32[768,512]{1,0:T(8,128)}, f32[768,512]{1,0:T(8,128)}) fusion(bf16[2,768,512]{2,1,0:T(8,128)(2,1)} %shard_map.77), kind=kLoop, calls=%fused_computation | loop fusion | flops 786432 | bytes 4718592 | tf_op jit(solution)/shard_map/convert_element_type | solution.py:391
